TPU v7x, 32 devices: a whole 2x2x4 slice. The times are simulated.
32 devices in a mesh: dp: 8 (over z, y), task: 4 (over x, core).
Axes of the slice: x: 2, y: 2, z: 4, core: 2. Of those that a mesh axis runs over, the one named last changes fastest.
Arguments:
- images: bfloat16 [32768, 2, 2, 512], P(('dp', 'task')), may hold values from -6 to 6
- image_counts: int32 [32], P(('dp', 'task')), may hold values from 341 to 1024, as said below
- labels: int32 [32768, 40], P(('dp', 'task')), may hold values from 0 to 1
- fw_picks: int32 [20], replicated, may hold values from 0 to 39
- task_average: float32 [40], replicated, may hold values from 0 to 1, as said below
- conv_weights: float32 [2, 4608, 512], P(None, ('dp', 'task')), may hold values from -0.09375 to 0.09375
- conv_momentum: float32 [2, 4608, 512], P(None, ('dp', 'task')), may hold values from -0.00015258789 to 0.00015258789
- conv_average: float32 [2, 4608, 512], P(None, ('dp', 'task')), may hold values from -0.09375 to 0.09375
- norm_parameter_list: float32 [4, 512], replicated, may hold values from -1.2 to 1.3
- norm_momentum: float32 [4, 512], replicated, may hold values from -0.00015258789 to 0.00015258789
- norm_average: float32 [4, 512], replicated, may hold values from -4 to 4
- head_params: float32 [513, 40], P(None, 'task'), may hold values from -6 to 6
- head_momentum: float32 [513, 40], P(None, 'task'), may hold values from -0.0008544922 to 0.0008544922
- head_average: float32 [513, 40], P(None, 'task'), may hold values from -4 to 4
Outputs:
- block_output: bfloat16 [32768, 2, 2, 512], P(('dp', 'task'))
- image_grad: float32 [32768, 2, 2, 512], P(('dp', 'task'))
- conv_grads: float32 [2, 4608, 512], P(None, ('dp', 'task'))
- conv_momentum_new: float32 [2, 4608, 512], P(None, ('dp', 'task'))
- conv_weights_new: float32 [2, 4608, 512], P(None, ('dp', 'task'))
- conv_average_new: float32 [2, 4608, 512], P(None, ('dp', 'task'))
- conv_weights_low: bfloat16 [2, 4608, 512], P(None, ('dp', 'task'))
- norm_grads: float32 [4, 512], replicated
- norm_momentum_new: float32 [4, 512], replicated
- norm_params_new: float32 [4, 512], replicated
- norm_average_new: float32 [4, 512], replicated
- head_grads: float32 [513, 40], P(None, 'task')
- head_momentum_new: float32 [513, 40], P(None, 'task')
- head_params_new: float32 [513, 40], P(None, 'task')
- head_average_new: float32 [513, 40], P(None, 'task')
- task_average_new: float32 [40], replicated
Inputs may be any that keep to these rules, and one draw needn't show every extreme that they name: Slot i of the d-th block of 1024 slots holds a real image when i < image_counts[d]; padded slots enter no statistic or loss. The last block is full. `task_average`: positive entries summing to one.
All inputs are finite; a program needn't handle non-finite values.
Results may differ from a plain program's by a relative error of at most 0.0035.
The roundings to bfloat16 on the way count: a program that leaves them out, or rounds other values in their place, can miss the bound.
Values may be sent and summed in bfloat16 or wider, within the bound.
No kernel may reach another device: no remote copies, remote signals or barrier semaphores. Data moves between devices by JAX's collectives and lax.ppermute only.
A program may use at most 192 MiB of HBM per device.

v0:
```python
import jax
import jax.numpy as jnp
from jax import lax
from jax.sharding import PartitionSpec as P

EPSILON = 1e-05
MOMENTUM_DECAY = 0.5
AVERAGE_DECAY = 0.5
CONV_RATE = 2000.0
NORM_RATE = 40000.0
HEAD_RATE = 1000.0
STEP_CAP = 0.5
PRECISE = lax.Precision.HIGHEST


def unfold(kernel, map_side):
    block_rows = []
    for in_row in range(map_side):
        for in_col in range(map_side):
            pieces = []
            for out_row in range(map_side):
                for out_col in range(map_side):
                    pieces.append(kernel[in_row - out_row + 1, in_col - out_col + 1])
            block_rows.append(jnp.concatenate(pieces, axis=1))
    return jnp.concatenate(block_rows, axis=0)


def fold(grad_matrix, map_side, channels):
    tap_sums = {}
    for in_row in range(map_side):
        for in_col in range(map_side):
            in_index = in_row * map_side + in_col
            for out_row in range(map_side):
                for out_col in range(map_side):
                    out_index = out_row * map_side + out_col
                    offset = (in_row - out_row + 1, in_col - out_col + 1)
                    block = grad_matrix[
                        in_index * channels : (in_index + 1) * channels,
                        out_index * channels : (out_index + 1) * channels,
                    ]
                    if offset in tap_sums:
                        tap_sums[offset] = tap_sums[offset] + block
                    else:
                        tap_sums[offset] = block
    stacked = []
    for kernel_row in range(3):
        for kernel_col in range(3):
            stacked.append(
                tap_sums.get((kernel_row, kernel_col), jnp.zeros((channels, channels), jnp.float32))
            )
    return jnp.stack(stacked).reshape(9 * channels, channels)


def apply_norm(values, value_sum, square_sum, spatial_positions):
    mean_value = value_sum / spatial_positions
    inverse_deviation = lax.rsqrt(
        square_sum / spatial_positions - mean_value * mean_value + EPSILON
    )
    return ((values - mean_value) * inverse_deviation, inverse_deviation)


def norm_backward(
    gradient_values,
    centered_scaled,
    inverse_deviation,
    norm_gain,
    norm_shift_gradient,
    norm_gain_gradient,
    weight_matrix_rows,
    spatial_positions,
):
    return (
        norm_gain
        * inverse_deviation
        * (
            gradient_values
            - weight_matrix_rows
            * (norm_shift_gradient + centered_scaled * norm_gain_gradient)
            / spatial_positions
        )
    )


def frank_wolfe(gram_matrix, start_mix, vertex_ids):
    task_ids = jnp.arange(gram_matrix.shape[0], dtype=jnp.int32)

    def frank_step(task_mix, vertex):
        corner = (task_ids == vertex).astype(gram_matrix.dtype)
        gram_mix = jnp.dot(gram_matrix, task_mix, precision=PRECISE)
        gram_corner = jnp.dot(gram_matrix, corner, precision=PRECISE)
        mix_mix = jnp.sum(task_mix * gram_mix)
        mix_corner = jnp.sum(corner * gram_mix)
        corner_corner = jnp.sum(corner * gram_corner)
        step_size = jnp.clip(
            (mix_mix - mix_corner) / (mix_mix - 2.0 * mix_corner + corner_corner), 0.0, STEP_CAP
        )
        return ((1.0 - step_size) * task_mix + step_size * corner, None)

    final_mix, unused = lax.scan(frank_step, start_mix, vertex_ids)
    return final_mix


def nesterov(params, momentum, grads, rate, average):
    momentum_new = MOMENTUM_DECAY * momentum + grads
    params_new = params - rate * (grads + MOMENTUM_DECAY * momentum_new)
    average_new = AVERAGE_DECAY * average + (1.0 - AVERAGE_DECAY) * params_new
    return (momentum_new, params_new, average_new)


def on_device(
    images,
    image_counts,
    labels,
    fw_picks,
    task_average,
    conv_weights,
    conv_momentum,
    conv_average,
    norm_parameter_list,
    norm_momentum,
    norm_average,
    head_params,
    head_momentum,
    head_average,
):
    row_count = images.shape[0]
    map_side = images.shape[1]
    channels = images.shape[3]
    positions_per = map_side * map_side
    gathered = lax.all_gather(conv_weights.astype(jnp.bfloat16), ("dp", "task"), axis=1, tiled=True)
    kernels = gathered.reshape(2, 3, 3, channels, channels)
    unfold_one = unfold(kernels[0], map_side)
    unfold_two = unfold(kernels[1], map_side)
    heads = lax.all_gather(head_params, "task", axis=1, tiled=True)
    head_rows = heads[:channels]
    own_count = image_counts[0]
    real_rows = (jnp.arange(row_count, dtype=jnp.int32) < own_count).astype(jnp.float32)
    weight_matrix_rows = real_rows[:, None, None]
    count_float = own_count.astype(jnp.float32)
    flat_images = images.reshape(row_count, positions_per * channels)
    first_moment = jnp.dot(flat_images, unfold_one, preferred_element_type=jnp.float32).reshape(
        row_count, positions_per, channels
    )
    first_moment_total = jnp.sum(first_moment * weight_matrix_rows, axis=(0, 1))
    first_moment_square = jnp.sum(first_moment * first_moment * weight_matrix_rows, axis=(0, 1))
    real_total = lax.psum(count_float, ("dp", "task"))
    first_moment_total, first_moment_square = lax.psum(
        (first_moment_total, first_moment_square), ("dp", "task")
    )
    spatial_positions = real_total * positions_per
    first_centered_scaled, first_inverse_deviation = apply_norm(
        first_moment, first_moment_total, first_moment_square, spatial_positions
    )
    first_normalized = norm_parameter_list[0] * first_centered_scaled + norm_parameter_list[1]
    hidden_act, gelu_one = jax.vjp(jax.nn.gelu, first_normalized)
    hidden = hidden_act.astype(jnp.bfloat16).reshape(row_count, positions_per * channels)
    second_moment = jnp.dot(hidden, unfold_two, preferred_element_type=jnp.float32).reshape(
        row_count, positions_per, channels
    )
    second_moment_total = jnp.sum(second_moment * weight_matrix_rows, axis=(0, 1))
    second_moment_square = jnp.sum(second_moment * second_moment * weight_matrix_rows, axis=(0, 1))
    second_moment_total, second_moment_square = lax.psum(
        (second_moment_total, second_moment_square), ("dp", "task")
    )
    second_centered_scaled, second_inverse_deviation = apply_norm(
        second_moment, second_moment_total, second_moment_square, spatial_positions
    )
    second_normalized = norm_parameter_list[2] * second_centered_scaled + norm_parameter_list[3]
    block_out, gelu_out = jax.vjp(
        jax.nn.gelu,
        second_normalized + images.reshape(row_count, positions_per, channels).astype(jnp.float32),
    )
    block_output = block_out.astype(jnp.bfloat16).reshape(images.shape)
    pooled = jnp.mean(block_out, axis=1)
    logits = jnp.dot(pooled, head_rows, precision=PRECISE) + heads[channels]
    resid = real_rows[:, None] * (jax.nn.sigmoid(logits) - labels.astype(jnp.float32)) / real_total
    partial_gram = jnp.dot(resid.T, resid, precision=PRECISE) * jnp.dot(
        head_rows.T, head_rows, precision=PRECISE
    )
    gram_matrix = lax.psum(partial_gram, ("dp", "task"))
    task_mix = frank_wolfe(gram_matrix, task_average, fw_picks)
    task_average_new = AVERAGE_DECAY * task_average + (1.0 - AVERAGE_DECAY) * task_mix
    weighted = resid * task_mix[None, :]
    head_partial = jnp.concatenate(
        [jnp.dot(pooled.T, weighted, precision=PRECISE), jnp.sum(weighted, axis=0)[None, :]], axis=0
    )
    pooled_grad = jnp.dot(weighted, head_rows.T, precision=PRECISE)
    out_grad = jnp.broadcast_to(pooled_grad[:, None, :] / positions_per, block_out.shape)
    prenorm_gradient = gelu_out(out_grad)[0]
    second_norm_shift = jnp.sum(prenorm_gradient, axis=(0, 1))
    second_norm_gain = jnp.sum(prenorm_gradient * second_centered_scaled, axis=(0, 1))
    second_norm_shift, second_norm_gain, head_sum = lax.psum(
        (second_norm_shift, second_norm_gain, head_partial), ("dp", "task")
    )
    second_grad = norm_backward(
        prenorm_gradient,
        second_centered_scaled,
        second_inverse_deviation,
        norm_parameter_list[2],
        second_norm_shift,
        second_norm_gain,
        weight_matrix_rows,
        spatial_positions,
    )
    second_grad = second_grad.astype(jnp.bfloat16).reshape(row_count, positions_per * channels)
    hidden_grad = jnp.dot(second_grad, unfold_two.T, preferred_element_type=jnp.float32)
    grad_two = fold(
        jnp.dot(hidden.T, second_grad, preferred_element_type=jnp.float32), map_side, channels
    )
    normalized_gradient = gelu_one(hidden_grad.reshape(row_count, positions_per, channels))[0]
    shift_one = jnp.sum(normalized_gradient, axis=(0, 1))
    first_norm_gain = jnp.sum(normalized_gradient * first_centered_scaled, axis=(0, 1))
    shift_one, first_norm_gain = lax.psum((shift_one, first_norm_gain), ("dp", "task"))
    first_grad = norm_backward(
        normalized_gradient,
        first_centered_scaled,
        first_inverse_deviation,
        norm_parameter_list[0],
        shift_one,
        first_norm_gain,
        weight_matrix_rows,
        spatial_positions,
    )
    first_grad = first_grad.astype(jnp.bfloat16).reshape(row_count, positions_per * channels)
    image_flat = jnp.dot(
        first_grad, unfold_one.T, preferred_element_type=jnp.float32
    ) + prenorm_gradient.reshape(row_count, positions_per * channels)
    image_grad = image_flat.reshape(images.shape)
    grad_one = fold(
        jnp.dot(flat_images.T, first_grad, preferred_element_type=jnp.float32), map_side, channels
    )
    local_grads = jnp.stack([grad_one, grad_two])
    shard_rows = conv_weights.shape[1]
    summed = lax.psum(local_grads, ("dp", "task"))
    conv_grads = lax.dynamic_slice_in_dim(
        summed, lax.axis_index(("dp", "task")) * shard_rows, shard_rows, 1
    )
    norm_grads = jnp.stack([first_norm_gain, shift_one, second_norm_gain, second_norm_shift])
    task_cols = head_params.shape[1]
    head_grads = lax.dynamic_slice_in_dim(
        head_sum, lax.axis_index("task") * task_cols, task_cols, 1
    )
    conv_momentum_new, conv_weights_new, conv_average_new = nesterov(
        conv_weights, conv_momentum, conv_grads, CONV_RATE, conv_average
    )
    norm_momentum_new, norm_params_new, norm_average_new = nesterov(
        norm_parameter_list, norm_momentum, norm_grads, NORM_RATE, norm_average
    )
    head_momentum_new, head_params_new, head_average_new = nesterov(
        head_params, head_momentum, head_grads, HEAD_RATE, head_average
    )
    return (
        block_output,
        image_grad,
        conv_grads,
        conv_momentum_new,
        conv_weights_new,
        conv_average_new,
        conv_weights_new.astype(jnp.bfloat16),
        norm_grads,
        norm_momentum_new,
        norm_params_new,
        norm_average_new,
        head_grads,
        head_momentum_new,
        head_params_new,
        head_average_new,
        task_average_new,
    )


def solution(mesh):
    return jax.shard_map(
        on_device,
        mesh=mesh,
        in_specs=(
            P(("dp", "task"), None, None, None),
            P(("dp", "task")),
            P(("dp", "task"), None),
            P(),
            P(),
            P(None, ("dp", "task"), None),
            P(None, ("dp", "task"), None),
            P(None, ("dp", "task"), None),
            P(),
            P(),
            P(),
            P(None, "task"),
            P(None, "task"),
            P(None, "task"),
        ),
        out_specs=(
            P(("dp", "task"), None, None, None),
            P(("dp", "task"), None, None, None),
            P(None, ("dp", "task"), None),
            P(None, ("dp", "task"), None),
            P(None, ("dp", "task"), None),
            P(None, ("dp", "task"), None),
            P(None, ("dp", "task"), None),
            P(),
            P(),
            P(),
            P(),
            P(None, "task"),
            P(None, "task"),
            P(None, "task"),
            P(None, "task"),
            P(),
        ),
        check_vma=False,
    )
```

profile of v0, /device:TPU:0, one launch (start us, length us, event | category | flops | bytes accessed | tf_op | source)
XLA Modules:
  0.0 1071.6 jit_solution(11733317102179793943)
XLA Ops:
  9.1 7.8 reshape.99
  16.9 12.4 %copy.114 = f32[1024,2,2,512]{0,3,2,1:T(8,128)} copy(bf16[1024,2,2,512]{3,2,1,0:T(2,128)(2,1)} %param.16) | data formatting | bytes 12582912 | tf_op jit(solution)/shard_map/convert_element_type | solution.py:171
  30.0 6.7 all-gather
  36.8 59.5 %all-gather.3.cloned.1.call-done = bf16[2,4608,512]{2,1,0:T(8,128)(2,1)} async-done(((bf16[2,144,512]{2,1,0:T(8,128)(2,1)}), bf16[2,4608,512]{2,1,0:T(8,128)(2,1)}) %all-gather.3.cloned.1.call-update) | async-done | bytes 9437200 | tf_op jit(solution)/shard_map/all_gather | solution.py:130
  96.3 6.6 fusion.120
  104.8 4.2 slice_bitcast_fusion.13
  122.5 47.1 %maximum_maximum_fusion.1 = bf16[2048,2048]{0,1:T(8,128)(2,1)} fusion(bf16[512,512]{0,1:T(8,128)(2,1)} %bitcast.244, bf16[512,512]{0,1:T(8,128)(2,1)} %bitcast.241, bf16[512,512]{0,1:T(8,128)(2,1)} %bitcast.239, bf16[512,512]{0,1:T(8,128)(2,1)S(1)} %bitcast.245, bf16[512,512]{0,1:T(8,128)(2,1)} %bitcast.243, bf16[512,512]{0,1:T(8,128)(2,1)} %bitcast.238, ...), kind=kLoop, calls=%fused_computation.42 | loop fusion | flops 134217728 | bytes 13107200 | tf_op jit(solution)/shard_map/concatenate | solution.py:25
  169.6 12.4 %copy.118 = bf16[2048,2048]{1,0:T(8,128)(2,1)} copy(bf16[2048,2048]{0,1:T(8,128)(2,1)} %maximum_maximum_fusion.1) | data formatting | bytes 16777216 | tf_op jit(solution)/shard_map/concatenate | solution.py:25
  182.0 38.4 %maximum_maximum_fusion = bf16[2048,2048]{1,0:T(8,128)(2,1)S(1)} fusion(bf16[512,512]{1,0:T(8,128)(2,1)} %get-tuple-element.193, bf16[512,512]{1,0:T(8,128)(2,1)} %get-tuple-element.190, bf16[512,512]{1,0:T(8,128)(2,1)} %get-tuple-element.188, bf16[512,512]{1,0:T(8,128)(2,1)S(1)} %get-tuple-element.186, bf16[512,512]{1,0:T(8,128)(2,1)} %get-tuple-element.192, ...), kind=kLoop, calls=%fused_computation.41 | loop fusion | flops 134217728 | bytes 13107200 | tf_op jit(solution)/shard_map/concatenate | solution.py:25
  220.4 16.6 %fusion.31 = (f32[2048]{0:T(1024)S(1)}, f32[2048]{0:T(1024)S(1)}, f32[2048,1024]{1,0:T(8,128)}) fusion(f32[1024]{0:T(1024)S(1)} %fusion.108, bf16[2048,2048]{1,0:T(8,128)(2,1)S(1)} %maximum_maximum_fusion, bf16[1024,2048]{1,0:T(8,128)(2,1)} %reshape.99), kind=kOutput, calls=%fused_computation.47 | convolution fusion | flops 8600416256 | bytes 20992000 | tf_op jit(solution)/shard_map/dot_general | solution.py:141
  237.1 39.4 %all-reduce.3 = (f32[512]{0:T(512)S(1)}, f32[]{:T(128)}, f32[512]{0:T(512)S(1)}) all-reduce(f32[512]{0:T(512)S(1)} %reduce_sum.136, f32[]{:T(128)S(6)} %convert_element_type.45, f32[512]{0:T(512)S(1)} %reduce_sum.133), channel_id=1, replica_groups=mesh['dp'=8,'task'=4] {'dp','task'}, use_global_device_ids=true, to_apply=%region_6.0 | all-reduce | flops 1025 | bytes 8200 | tf_op jit(solution)/shard_map/psum | solution.py:147
  277.2 20.8 %multiply_reduce_fusion.4 = (f32[512]{0:T(512)S(1)}, f32[512]{0:T(512)S(1)}, f32[1024,4,512]{0,2,1:T(8,128)}) fusion(f32[1024]{0:T(1024)S(1)} %fusion.108, bf16[4,512,2048]{2,1,0:T(8,128)(2,1)} %bitcast.222, f32[2048]{0:T(1024)S(1)} %bitcast.261, f32[2048]{0:T(1024)S(1)} %bitcast.265, f32[2048]{0:T(1024)S(1)} %bitcast.267, ...), kind=kOutput, calls=%fused_computation.62 | convolution fusion | flops 8627683328 | bytes 25206784 | tf_op jit(solution)/shard_map/dot_general | solution.py:157
  298.0 40.2 %all-reduce.2 = (f32[512]{0:T(512)S(1)}, f32[512]{0:T(512)S(1)}) all-reduce(f32[512]{0:T(512)S(1)} %get-tuple-element.137, f32[512]{0:T(512)S(1)} %get-tuple-element.136), channel_id=1, replica_groups=mesh['dp'=8,'task'=4] {'dp','task'}, use_global_device_ids=true, to_apply=%region_10.0 | all-reduce | flops 1024 | bytes 8192 | tf_op jit(solution)/shard_map/psum | solution.py:162
  338.3 11.6 %fusion.40 = (f32[1024,512]{0,1:T(8,128)}, f32[1024,4,512]{0,2,1:T(8,128)}) fusion(f32[1024,2,2,512]{0,3,2,1:T(8,128)} %copy.114, f32[512]{0:T(512)S(1)} %bitcast.260, f32[512]{0:T(512)S(1)} %get-tuple-element.178, f32[1024,4,512]{0,2,1:T(8,128)} %get-tuple-element.212, f32[512]{0:T(512)S(1)} %get-tuple-element.209, f32[512]{0:T(512)S(1)} %bitcast.252), kind=kLoop, calls=%fused_computation.65 | loop fusion | flops 28835840 | bytes 27271168 | tf_op jit(solution)/shard_map/reduce_sum | solution.py:174
  355.1 40.2 %psum.89 = f32[40,40]{1,0:T(8,128)S(1)} all-reduce(f32[40,40]{1,0:T(8,128)S(1)} %convolution_multiply_fusion), channel_id=1, replica_groups=mesh['dp'=8,'task'=4] {'dp','task'}, use_global_device_ids=true, to_apply=%region_12.0 | all-reduce | flops 1600 | bytes 12800 | tf_op jit(solution)/shard_map/psum | solution.py:180
  395.3 146.5 %while.11 = (s32[]{:T(128)}, f32[40]{0:T(128)S(1)}, f32[40,40]{1,0:T(8,128)S(1)}, s32[20]{0:T(128)S(1)}, s32[]{:T(128)}, /*index=5*/f32[]{:T(128)}, f32[]{:T(128)}, f32[]{:T(128)}, f32[]{:T(128)}) while((s32[]{:T(128)}, f32[40]{0:T(128)S(1)}, f32[40,40]{1,0:T(8,128)S(1)}, s32[20]{0:T(128)S(1)}, s32[]{:T(128)}, ...), condition=%wide.region_17.18_spmd.clone, body=%wide.region_13.17_spmd.clone.sunk | while | flops 38927 | bytes 13521 | solution.py:99
  543.5 4.1 broadcast_multiply_fusion
  549.5 3.0 copy.117
  552.5 15.0 %fusion.115 = (f32[512]{0:T(512)S(1)}, f32[512]{0:T(512)S(1)}, f32[1024,4,512]{0,2,1:T(8,128)}, bf16[1024,4,512]{0,2,1:T(8,128)(2,1)}) fusion(f32[512]{0:T(512)S(1)} %get-tuple-element.178, f32[1024,4,512]{0,2,1:T(8,128)} %get-tuple-element.212, f32[512]{0:T(512)S(1)} %get-tuple-element.209, f32[1024,4,512]{0,2,1:T(8,128)} %get-tuple-element.181, ...), kind=kLoop, calls=%fused_computation.184 | loop fusion | flops 54524928 | bytes 33562624 | tf_op jit(solution)/shard_map/reduce_sum | solution.py:190
  567.5 40.4 %all-reduce.1 = (f32[512]{0:T(512)S(1)}, f32[512]{0:T(512)S(1)}) all-reduce(f32[512]{0:T(512)S(1)} %get-tuple-element.143, f32[512]{0:T(512)S(1)} %get-tuple-element.142), channel_id=1, replica_groups=mesh['dp'=8,'task'=4] {'dp','task'}, use_global_device_ids=true, to_apply=%region_21.22 | all-reduce | flops 1024 | bytes 8192 | tf_op jit(solution)/shard_map/psum | solution.py:192
  607.9 7.5 multiply_convert_fusion.1
  615.5 16.9 %fusion.111 = f32[2048,2048]{1,0:T(8,128)} fusion(bf16[1024,2048]{0,1:T(8,128)(2,1)S(1)} %bitcast.235, f32[2048,1024]{1,0:T(8,128)} %get-tuple-element.211, f32[2048]{0:T(1024)S(1)} %bitcast.262, f32[2048]{0:T(1024)S(1)} %bitcast.266, f32[2048]{0:T(1024)S(1)} %bitcast.268, f32[2048]{0:T(1024)S(1)} %bitcast.264), kind=kOutput, calls=%fused_computation.182 | convolution fusion | flops 8617197568 | bytes 29392896 | tf_op jit(solution)/shard_map/dot_general | solution.py:208
  632.4 18.8 %fusion.114 = (f32[512]{0:T(512)S(1)}, f32[512]{0:T(512)S(1)}, f32[1024,4,512]{0,2,1:T(8,128)}) fusion(f32[512]{0:T(512)S(1)} %get-tuple-element.176, f32[1024,4,512]{0,2,1:T(8,128)} %bitcast.232, f32[512]{0:T(512)S(1)} %get-tuple-element.210, f32[512]{0:T(512)S(1)} %bitcast.270, f32[512]{0:T(512)S(1)} %bitcast.255, ...), kind=kOutput, calls=%fused_computation.183 | convolution fusion | flops 8644460544 | bytes 29372416 | tf_op jit(solution)/shard_map/dot_general | solution.py:206
  651.2 40.1 %all-reduce = (f32[512]{0:T(512)S(1)}, f32[512]{0:T(512)S(1)}) all-reduce(f32[512]{0:T(512)S(1)} %get-tuple-element.141, f32[512]{0:T(512)S(1)} %get-tuple-element.140), channel_id=1, replica_groups=mesh['dp'=8,'task'=4] {'dp','task'}, use_global_device_ids=true, to_apply=%region_25.26 | all-reduce | flops 1024 | bytes 8192 | tf_op jit(solution)/shard_map/psum | solution.py:213
  691.3 7.4 multiply_convert_fusion
  698.8 15.7 %convolution_bitcast_fusion.2 = f32[2048,2048]{1,0:T(8,128)} fusion(bf16[1024,2048]{0,1:T(8,128)(2,1)S(1)} %bitcast.233, bf16[1024,2048]{1,0:T(8,128)(2,1)} %reshape.99), kind=kOutput, calls=%fused_computation.20 | convolution fusion | flops 8589934592 | bytes 25165824 | tf_op jit(solution)/shard_map/dot_general | solution.py:230
  740.8 11.2 %pad_maximum_fusion = f32[2,4608,512]{2,1,0:T(8,128)} fusion(f32[1,4608,512]{2,1,0:T(8,128)} %bitcast.60, f32[1,4608,512]{2,1,0:T(8,128)S(1)} %bitcast.228), kind=kLoop, calls=%fused_computation.14 | loop fusion | flops 4718592 | bytes 37748736 | tf_op jit(solution)/shard_map/stack | solution.py:232
  752.0 11.3 %copy.122 = bf16[1024,2,2,512]{3,2,1,0:T(2,128)(2,1)} copy(bf16[1024,2,2,512]{0,3,2,1:T(8,128)(2,1)} %bitcast.227) | data formatting | bytes 8388608
  763.3 9.3 copy.120
  772.6 16.4 %convolution_add_fusion = f32[1024,2048]{1,0:T(8,128)} fusion(f32[1024,2048]{1,0:T(8,128)} %copy.120, bf16[1024,2048]{0,1:T(8,128)(2,1)} %bitcast.234, bf16[2048,2048]{1,0:T(8,128)(2,1)} %copy-done), kind=kOutput, calls=%fused_computation.67 | convolution fusion | flops 8592031744 | bytes 29360128 | tf_op jit(solution)/shard_map/dot_general | solution.py:225
  789.0 12.0 %reshape.105 = f32[1024,2,2,512]{3,2,1,0:T(2,128)} reshape(f32[1024,2048]{1,0:T(8,128)} %convolution_add_fusion) | data formatting | bytes 16777216 | tf_op jit(solution)/shard_map/reshape | solution.py:228
  802.1 257.5 %all-reduce.7.cloned.1.call-done = (f32[2,4608,512]{2,1,0:T(8,128)}, f32[513,40]{0,1:T(8,128)}) async-done(((f32[2,4608,512]{2,1,0:T(8,128)}, f32[513,40]{0,1:T(8,128)}), (f32[2,4608,512]{2,1,0:T(8,128)}, f32[513,40]{0,1:T(8,128)})) %all-reduce.7.cloned.1.call-update) | async-done | bytes 18956464 | tf_op jit(solution)/shard_map/psum | solution.py:234
  (198 shorter events, 139.4 us)
Async XLA Ops:
  7.2 89.1 %all-gather.3.cloned.1.call-start = ((), (), s32[]{:S(2)}) async-start(), calls=%async_computation | async-start | bytes 9732096 | tf_op jit(solution)/shard_map/all_gather | solution.py:130
  9.1 1050.6 %all-reduce.7.cloned.1.call-start = ((), (), s32[]{:S(2)}) async-start(), calls=%async_computation.1 | async-start | bytes 37953536 | tf_op jit(solution)/shard_map/psum | solution.py:234
  16.9 13.1 %copy-start.15 = (f32[4,512]{1,0:T(4,128)S(1)}, f32[4,512]{1,0:T(4,128)}, u32[]{:S(2)}) copy-start(f32[4,512]{1,0:T(4,128)} %param.24) | copy-start | bytes 24580
  16.9 13.1 %copy-start.7 = (f32[513,10]{0,1:T(8,128)S(1)}, f32[513,10]{0,1:T(8,128)}, u32[]{:S(2)}) copy-start(f32[513,10]{0,1:T(8,128)} %param.27) | copy-start | bytes 61564
  220.4 16.6 %copy-start = (bf16[2048,2048]{1,0:T(8,128)(2,1)}, bf16[2048,2048]{1,0:T(8,128)(2,1)S(1)}, u32[]{:S(2)}) copy-start(bf16[2048,2048]{1,0:T(8,128)(2,1)S(1)} %maximum_maximum_fusion) | copy-start | bytes 25165828
  338.3 13.6 %copy-start.6 = (s32[1024,40]{0,1:T(8,128)S(1)}, s32[1024,40]{0,1:T(8,128)}, u32[]{:S(2)}) copy-start(s32[1024,40]{0,1:T(8,128)} %param.18) | copy-start | bytes 491524
  338.3 57.0 %copy-start.12 = (f32[40]{0:T(128)S(1)}, f32[40]{0:T(128)}, u32[]{:S(2)}) copy-start(f32[40]{0:T(128)} %param.20) | copy-start | bytes 484
  338.3 57.0 %copy-start.19 = (s32[20]{0:T(128)S(1)}, s32[20]{0:T(128)}, u32[]{:S(2)}) copy-start(s32[20]{0:T(128)} %param.19) | copy-start | bytes 244
  541.8 25.7 %copy-start.10 = (f32[40]{0:T(128)}, f32[40]{0:T(128)S(1)}, u32[]{:S(2)}) copy-start(f32[40]{0:T(128)S(1)} %get-tuple-element.43) | copy-start | bytes 484
  607.9 24.5 %slice-start.4 = ((s8[8388608]{0:T(1024)(128)(4,1)}), s8[4194304]{0:T(1024)(128)(4,1)S(1)}, s32[]{:S(2)}) async-start(s8[8388608]{0:T(1024)(128)(4,1)} %bitcast.229), calls=%async_computation.6 | async-start | bytes 8388608
  615.5 16.9 %slice-start.5 = ((s8[8388608]{0:T(1024)(128)(4,1)}), s8[4194304]{0:T(1024)(128)(4,1)S(1)}, s32[]{:S(2)}) async-start(s8[8388608]{0:T(1024)(128)(4,1)} %bitcast.229), calls=%async_computation.7 | async-start | bytes 8388608
  698.7 15.8 %copy-start.1 = (bf16[1024,4,512]{0,2,1:T(8,128)(2,1)}, bf16[1024,4,512]{0,2,1:T(8,128)(2,1)S(1)}, u32[]{:S(2)}) copy-start(bf16[1024,4,512]{0,2,1:T(8,128)(2,1)S(1)} %multiply_convert_fusion) | copy-start | bytes 12582916
  698.7 30.8 %slice-start = ((s8[16777216]{0:T(1024)(128)(4,1)}), s8[4194304]{0:T(1024)(128)(4,1)S(1)}, s32[]{:S(2)}) async-start(s8[16777216]{0:T(1024)(128)(4,1)} %bitcast.225), calls=%async_computation.2 | async-start | bytes 8388608
  698.7 30.8 %slice-start.1 = ((s8[16777216]{0:T(1024)(128)(4,1)}), s8[4194304]{0:T(1024)(128)(4,1)S(1)}, s32[]{:S(2)}) async-start(s8[16777216]{0:T(1024)(128)(4,1)} %bitcast.225), calls=%async_computation.3 | async-start | bytes 8388608
  698.8 30.8 %slice-start.2 = ((s8[16777216]{0:T(1024)(128)(4,1)}), s8[4194304]{0:T(1024)(128)(4,1)S(1)}, s32[]{:S(2)}) async-start(s8[16777216]{0:T(1024)(128)(4,1)} %bitcast.225), calls=%async_computation.4 | async-start | bytes 8388608
  715.8 13.8 %slice-start.3 = ((s8[16777216]{0:T(1024)(128)(4,1)}), s8[4194304]{0:T(1024)(128)(4,1)S(1)}, s32[]{:S(2)}) async-start(s8[16777216]{0:T(1024)(128)(4,1)} %bitcast.225), calls=%async_computation.5 | async-start | bytes 8388608
  788.9 12.1 %copy-start.9 = (f32[40]{0:T(128)S(1)}, f32[40]{0:T(128)}, u32[]{:S(2)}) copy-start(f32[40]{0:T(128)} %param.20) | copy-start | bytes 484
  788.9 12.1 %copy-start.11 = (f32[40]{0:T(128)S(1)}, f32[40]{0:T(128)}, u32[]{:S(2)}) copy-start(f32[40]{0:T(128)} %copy-done.10) | copy-start | bytes 484
  788.9 12.6 %copy-start.16 = (f32[4,512]{1,0:T(4,128)S(1)}, f32[4,512]{1,0:T(4,128)}, u32[]{:S(2)}) copy-start(f32[4,512]{1,0:T(4,128)} %param.24) | copy-start | bytes 24580
  788.9 12.6 %copy-start.17 = (f32[4,512]{1,0:T(4,128)S(1)}, f32[4,512]{1,0:T(4,128)}, u32[]{:S(2)}) copy-start(f32[4,512]{1,0:T(4,128)} %param.26) | copy-start | bytes 24580
  788.9 12.6 %copy-start.18 = (f32[4,512]{1,0:T(4,128)S(1)}, f32[4,512]{1,0:T(4,128)}, u32[]{:S(2)}) copy-start(f32[4,512]{1,0:T(4,128)} %param.25) | copy-start | bytes 24580
  789.0 270.7 %copy-start.3 = (f32[2,144,512]{2,1,0:T(8,128)S(1)}, f32[2,144,512]{2,1,0:T(8,128)}, u32[]{:S(2)}) copy-start(f32[2,144,512]{2,1,0:T(8,128)} %param.21) | copy-start | bytes 1769476
  789.0 270.7 %copy-start.5 = (f32[2,144,512]{2,1,0:T(8,128)S(1)}, f32[2,144,512]{2,1,0:T(8,128)}, u32[]{:S(2)}) copy-start(f32[2,144,512]{2,1,0:T(8,128)} %param.22) | copy-start | bytes 1769476
  789.0 273.0 %copy-start.4 = (f32[2,144,512]{2,1,0:T(8,128)S(1)}, f32[2,144,512]{2,1,0:T(8,128)}, u32[]{:S(2)}) copy-start(f32[2,144,512]{2,1,0:T(8,128)} %param.23) | copy-start | bytes 1769476
  789.0 274.0 %copy-start.8 = (f32[513,10]{0,1:T(8,128)S(1)}, f32[513,10]{0,1:T(8,128)}, u32[]{:S(2)}) copy-start(f32[513,10]{0,1:T(8,128)} %param.27) | copy-start | bytes 61564
  789.0 274.0 %copy-start.13 = (f32[513,10]{0,1:T(8,128)S(1)}, f32[513,10]{0,1:T(8,128)}, u32[]{:S(2)}) copy-start(f32[513,10]{0,1:T(8,128)} %param.29) | copy-start | bytes 61564
  789.0 274.0 %copy-start.14 = (f32[513,10]{0,1:T(8,128)S(1)}, f32[513,10]{0,1:T(8,128)}, u32[]{:S(2)}) copy-start(f32[513,10]{0,1:T(8,128)} %param.28) | copy-start | bytes 61564
  1062.0 2.5 copy-start.2
Sparse Core Ops, SparseCore 0:
  11.5 84.7 all-gather.2
  752.1 307.4 all-reduce.6
where the time goes:
time: 1080 us; the launch traced here: 1070 us
  waiting for transfers between devices  317 us (29%)
  blocking collectives  207 us (19%)
  other arithmetic  176 us (16%)
  matrix products  170 us (16%)
  local copies, waits for them, and re-layouts  120 us (11%)
  loops' own time  65.9 us (6%)
  between operations  16.1 us (1%)
    psum x1, waiting for transfers between devices, on_device(): summed = lax.psum(local_grads, ('dp', 'task'))  258 us
    concatenate x2, other arithmetic, unfold(): return jnp.concatenate(block_rows, axis=0)  85.5 us
    another operation x1, loops' own time, frank_wolfe(): final_mix, unused = lax.scan(frank_step, start_mix, vertex_ids)  65.9 us
    all_gather x1, waiting for transfers between devices, on_device(): lax.all_gather(conv_weights.astype(jnp.bfloat16), ('dp', 'task'), axis=1,...  59.5 us
    psum x1, blocking collectives, on_device(): lax.psum((second_norm_shift, second_norm_gain, head_partial), ('dp', 'tas...  40.4 us
    psum x1, blocking collectives, on_device(): lax.psum((second_moment_total, second_moment_square), ('dp', 'task'))  40.2 us
    psum x1, blocking collectives, on_device(): gram_matrix = lax.psum(partial_gram, ('dp', 'task'))  40.2 us
    psum x1, blocking collectives, on_device(): lax.psum((shift_one, first_norm_gain), ('dp', 'task'))  40.1 us
  transfers between devices with their start and end apart: 2, of which 2 were waited for; matrix products, arithmetic and copies ran while one was open for 7% of the time, Pallas kernels for 0%

commit v1 on v0

v1 whole, which is shorter than its diff:
```python
import jax
import jax.numpy as jnp
from jax import lax
from jax.experimental import pallas as pl
from jax.experimental.pallas import tpu as pltpu
from jax.sharding import PartitionSpec as P

EPSILON = 1e-05
MOMENTUM_DECAY = 0.5
AVERAGE_DECAY = 0.5
CONV_RATE = 2000.0
NORM_RATE = 40000.0
HEAD_RATE = 1000.0
STEP_CAP = 0.5
GELU_A = 0.7978845608
GELU_B = 0.7978845608 * 0.044715
AXES = ("dp", "task")
PRECISE = lax.Precision.HIGHEST
F32 = jnp.float32
BF16 = jnp.bfloat16
TILE = 256
LANES = 128
PARAMS = pltpu.CompilerParams(vmem_limit_bytes=58 << 20)


def tap(q, p):
    return (q // 2 - p // 2 + 1) * 3 + (q % 2 - p % 2 + 1)


def dot(a, b):
    return jnp.dot(a, b, preferred_element_type=F32)


def dot_nt(a, b):
    return lax.dot_general(a, b, (((1,), (1,)), ((), ())), preferred_element_type=F32)


def dot_tn(a, b):
    return lax.dot_general(a, b, (((0,), (0,)), ((), ())), preferred_element_type=F32)


def precise(a, b, dims):
    return lax.dot_general(a, b, ((dims[0], dims[1]), ((), ())), precision=PRECISE, preferred_element_type=F32)


def fold8(v):
    return jnp.sum(v.reshape(v.shape[0] // 8, 8, v.shape[1]), 0)


def spread_rows(out_ref, rows):
    line = 0
    for row in rows:
        for j in range(row.shape[1] // LANES):
            part = row[:, j * LANES : (j + 1) * LANES]
            out_ref[:, line : line + 1, :] = jnp.broadcast_to(part[None], (out_ref.shape[0], 1, LANES))
            line += 1


def gathered_rows(ref, count):
    total = jnp.sum(ref[...], 0)
    return [
        jnp.concatenate([total[4 * r + j : 4 * r + j + 1, :] for j in range(4)], axis=1)
        for r in range(count)
    ], total


def moments(gathered_ref, spatial):
    (value_sum, square_sum), _ = gathered_rows(gathered_ref, 2)
    mean = value_sum / spatial
    inverse = lax.rsqrt(square_sum / spatial - mean * mean + EPSILON)
    return mean, inverse


def real_mask(count, rows):
    index = lax.broadcasted_iota(jnp.int32, (rows, 1), 0) + pl.program_id(0) * rows
    return (index < count).astype(F32)


def conv_rows(x_ref, k_ref, p):
    pr, pc = p // 2, p % 2
    acc = None
    for qr in range(2):
        base = ((qr - pr + 1) * 3 + (1 - pc)) * 512
        t = dot(x_ref[:, qr * 1024 : (qr + 1) * 1024], k_ref[base : base + 1024, :])
        acc = t if acc is None else acc + t
    return acc


def conv_stats(x_ref, k_ref, out_ref, mask):
    total = square = None
    for p in range(4):
        acc = conv_rows(x_ref, k_ref, p)
        out_ref[:, p * 512 : (p + 1) * 512] = acc
        masked = acc * mask
        s, q = fold8(masked), fold8(masked * acc)
        total = s if total is None else total + s
        square = q if square is None else square + q
    return total, square


def accumulate(step, steps, acc_ref, values, finish):
    @pl.when(step == 0)
    def _():
        for i, v in enumerate(values):
            acc_ref[i] = v

    @pl.when(step > 0)
    def _():
        for i, v in enumerate(values):
            acc_ref[i] += v

    @pl.when(step == steps - 1)
    def _():
        finish([jnp.sum(acc_ref[i], 0, keepdims=True) for i in range(len(values))])


def first_kernel(steps, count_ref, x_ref, k_ref, first_ref, stat_ref, acc_ref):
    step = pl.program_id(0)
    count = count_ref[0]
    values = conv_stats(x_ref, k_ref, first_ref, real_mask(count, TILE))

    def finish(rows):
        spread_rows(stat_ref, rows)
        stat_ref[:, 8:16, :] = jnp.full((stat_ref.shape[0], 8, LANES), count.astype(F32), F32)

    accumulate(step, steps, acc_ref, values, finish)


def gelu_tanh(v):
    return jnp.tanh(v * (GELU_A + GELU_B * (v * v)))


def gelu_slope(v, t):
    return (0.5 + 0.5 * t) + (0.5 * v) * (1.0 - t * t) * (GELU_A + (3.0 * GELU_B) * (v * v))


def second_kernel(steps, count_ref, first_ref, g1_ref, norm_ref, k_ref, hidden_ref, second_ref, stat_ref, acc_ref):
    step = pl.program_id(0)
    spatial = jnp.sum(g1_ref[:, 8:9, :], 0) * 4.0
    mean, inverse = moments(g1_ref, spatial[0:1, 0:1])
    scale = norm_ref[0:1, :] * inverse
    shift = norm_ref[1:2, :] - mean * scale
    for p in range(4):
        v = first_ref[:, p * 512 : (p + 1) * 512] * scale + shift
        half = 0.5 * v
        hidden_ref[:, p * 512 : (p + 1) * 512] = (half + half * gelu_tanh(v)).astype(BF16)
    values = conv_stats(hidden_ref, k_ref, second_ref, real_mask(count_ref[0], TILE))
    accumulate(step, steps, acc_ref, values, lambda rows: spread_rows(stat_ref, rows))


def head_kernel(
    steps, tasks, count_ref, second_ref, g2_ref, g1_ref, norm_ref, image_ref, label_ref, head_ref, pick_ref,
    out_ref, slope_ref, slope_sum_ref, slope_xhat_ref, pooled_ref, resid_ref, gram_out_ref, gram_ref,
):
    step = pl.program_id(0)
    real_total = jnp.sum(g1_ref[:, 8:9, :], 0)[0:1, 0:1]
    mean, inverse = moments(g2_ref, real_total * 4.0)
    gain, shift = norm_ref[2:3, :], norm_ref[3:4, :]
    pooled = slope_sum = slope_xhat = None
    for p in range(4):
        cols = slice(p * 512, (p + 1) * 512)
        xhat = (second_ref[:, cols] - mean) * inverse
        pre = gain * xhat + shift + image_ref[:, cols].astype(F32)
        t = gelu_tanh(pre)
        half = 0.5 * pre
        out = half + half * t
        out_ref[:, cols] = out.astype(BF16)
        slope = gelu_slope(pre, t)
        slope_ref[:, cols] = slope
        pooled = out if pooled is None else pooled + out
        slope_sum = slope if slope_sum is None else slope_sum + slope
        slope_xhat = slope * xhat if slope_xhat is None else slope_xhat + slope * xhat
    pooled = pooled * 0.25
    slope_sum_ref[...] = slope_sum
    slope_xhat_ref[...] = slope_xhat
    pooled_ref[:, 0:512] = pooled
    pooled_ref[:, 512:640] = (lax.broadcasted_iota(jnp.int32, (TILE, LANES), 1) == 0).astype(F32)
    logits = precise(pooled, head_ref[0:512, :], ((1,), (0,))) + head_ref[512:513, :]
    lane_real = (lax.broadcasted_iota(jnp.int32, (1, LANES), 1) < tasks).astype(F32)
    resid = (real_mask(count_ref[0], TILE) * lane_real) * (jax.nn.sigmoid(logits) - label_ref[...].astype(F32)) / real_total
    resid_ref[...] = resid
    part = precise(resid, resid, ((0,), (0,)))

    @pl.when(step == 0)
    def _():
        gram_ref[...] = part

    @pl.when(step > 0)
    def _():
        gram_ref[...] += part

    @pl.when(step == steps - 1)
    def _():
        heads = head_ref[0:512, :]
        gram = gram_ref[...] * precise(heads, heads, ((0,), (0,)))
        basis = pick_ref[...]
        projected = precise(gram, basis, ((1,), (1,)))
        lane = lax.broadcasted_iota(jnp.int32, (32, LANES), 1)
        row = lax.broadcasted_iota(jnp.int32, (32, LANES), 0)
        packed = None
        for group in range(3):
            placed = precise(projected, (lane == row + 32 * group).astype(F32), ((1,), (0,)))
            rows = precise(basis[8 * group : 8 * group + 8, :], placed, ((1,), (0,)))
            packed = rows if packed is None else packed + rows
        gram_out_ref[...] = jnp.broadcast_to(packed[None], gram_out_ref.shape)


def frank_wolfe(packed, picks, start_mix, fw_steps):
    rows = jnp.concatenate([packed[:, 32 * g : 32 * g + 32] for g in range(3)], axis=0)
    column = [jnp.broadcast_to(rows[:, k : k + 1], (24, LANES)) for k in range(fw_steps + 1)]
    along = column[fw_steps]
    a = along[fw_steps : fw_steps + 1, :]
    mix = start_mix
    for k in range(fw_steps):
        b = along[k : k + 1, :]
        c = column[k][k : k + 1, :]
        size = jnp.clip((a - b) / (a - 2.0 * b + c), 0.0, STEP_CAP)
        keep = 1.0 - size
        a = keep * keep * a + 2.0 * (keep * size) * b + size * size * c
        along = keep * along + size * column[k]
        mix = keep * mix + size * picks[k : k + 1, :]
    return mix


def mix_kernel(
    steps, fw_steps, gram_ref, pick_ref, start_ref, resid_ref, pooled_ref, head_ref, slope_sum_ref, slope_xhat_ref,
    dout_ref, stat_ref, head_grad_ref, mix_ref, acc_ref,
):
    step = pl.program_id(0)

    @pl.when(step == 0)
    def _():
        packed = jnp.sum(gram_ref[...], 0)
        start = start_ref[0:1, :]
        mix = frank_wolfe(packed, pick_ref[...], start, fw_steps)
        mix_ref[...] = jnp.broadcast_to(mix, mix_ref.shape)

    weighted = resid_ref[...] * mix_ref[0:1, :]
    dout = precise(weighted, head_ref[0:512, :], ((1,), (1,))) * 0.25
    dout_ref[...] = dout
    part = precise(weighted, pooled_ref[...], ((0,), (0,)))

    @pl.when(step == 0)
    def _():
        head_grad_ref[...] = part

    @pl.when(step > 0)
    def _():
        head_grad_ref[...] += part

    values = (fold8(dout * slope_xhat_ref[...]), fold8(dout * slope_sum_ref[...]))
    accumulate(step, steps, acc_ref, values, lambda rows: spread_rows(stat_ref, rows))


def back_second_kernel(
    steps, count_ref, slope_ref, dout_ref, second_ref, first_ref, g1_ref, g2_ref, g4_ref, norm_ref, k_ref,
    dsecond_ref, dnormed_ref, stat_ref, acc_ref,
):
    step = pl.program_id(0)
    spatial = jnp.sum(g1_ref[:, 8:9, :], 0)[0:1, 0:1] * 4.0
    mean1, inverse1 = moments(g1_ref, spatial)
    mean2, inverse2 = moments(g2_ref, spatial)
    (gain_grad, shift_grad), _ = gathered_rows(g4_ref, 2)
    scale2 = norm_ref[2:3, :] * inverse2
    by_value = scale2 * gain_grad * inverse2 / spatial
    by_one = scale2 * shift_grad / spatial - by_value * mean2
    mask = real_mask(count_ref[0], TILE)
    dout = dout_ref[...] * scale2
    real_value, real_one = mask * by_value, mask * by_one
    for p in range(4):
        cols = slice(p * 512, (p + 1) * 512)
        grad = dout * slope_ref[:, cols] - (real_one + real_value * second_ref[:, cols])
        dsecond_ref[:, cols] = grad.astype(BF16)
    gain1, shift1 = norm_ref[0:1, :], norm_ref[1:2, :]
    gain_sum = shift_sum = None
    for q in range(4):
        cols = slice(q * 512, (q + 1) * 512)
        acc = None
        for p in range(4):
            base = tap(q, p) * 512
            t = dot_nt(dsecond_ref[:, p * 512 : (p + 1) * 512], k_ref[base : base + 512, :])
            acc = t if acc is None else acc + t
        xhat = (first_ref[:, cols] - mean1) * inverse1
        v = gain1 * xhat + shift1
        dnormed = acc * gelu_slope(v, gelu_tanh(v))
        dnormed_ref[:, cols] = dnormed
        g, s = fold8(dnormed * xhat), fold8(dnormed)
        gain_sum = g if gain_sum is None else gain_sum + g
        shift_sum = s if shift_sum is None else shift_sum + s
    accumulate(step, steps, acc_ref, (gain_sum, shift_sum), lambda rows: spread_rows(stat_ref, rows))


def add_taps(out_ref, x_ref, value, p, seen):
    for q in range(4):
        index = tap(q, p)
        part = dot_tn(x_ref[:, q * 512 : (q + 1) * 512], value)
        rows = slice(index * 512, (index + 1) * 512)
        if index in seen:
            out_ref[rows, :] += part
        else:
            out_ref[rows, :] = part
        seen.add(index)


def weight_grad_kernel(x_ref, d0_ref, d1_ref, d2_ref, d3_ref, out_ref):
    seen = set()
    for p, ref in enumerate((d0_ref, d1_ref, d2_ref, d3_ref)):
        add_taps(out_ref, x_ref, ref[...], p, seen)


def dfirst_kernel(count_ref, dnormed_ref, first_ref, g1_ref, g5_ref, norm_ref, dfirst_ref):
    spatial = jnp.sum(g1_ref[:, 8:9, :], 0)[0:1, 0:1] * 4.0
    mean1, inverse1 = moments(g1_ref, spatial)
    (gain_grad, shift_grad), _ = gathered_rows(g5_ref, 2)
    scale = norm_ref[0:1, :] * inverse1
    by_value = scale * gain_grad * inverse1 / spatial
    by_one = scale * shift_grad / spatial - by_value * mean1
    mask = real_mask(count_ref[0], TILE)
    real_value, real_one = mask * by_value, mask * by_one
    for p in range(4):
        cols = slice(p * 512, (p + 1) * 512)
        grad = scale * dnormed_ref[:, cols] - (real_one + real_value * first_ref[:, cols])
        dfirst_ref[:, cols] = grad.astype(BF16)


def image_grad_kernel(dfirst_ref, k_ref, slope_ref, dout_ref, out_ref):
    dout = dout_ref[...]
    for q in range(4):
        cols = slice(q * 512, (q + 1) * 512)
        acc = dout * slope_ref[:, cols]
        for p in range(4):
            base = tap(q, p) * 512
            acc = acc + dot_nt(dfirst_ref[:, p * 512 : (p + 1) * 512], k_ref[base : base + 512, :])
        out_ref[:, cols] = acc


def nesterov(params, momentum, grads, rate, average):
    momentum_new = MOMENTUM_DECAY * momentum + grads
    params_new = params - rate * (grads + MOMENTUM_DECAY * momentum_new)
    average_new = AVERAGE_DECAY * average + (1.0 - AVERAGE_DECAY) * params_new
    return (momentum_new, params_new, average_new)


def shape(dims, dtype=F32):
    return jax.ShapeDtypeStruct(dims, dtype)


def whole(dims):
    return pl.BlockSpec(dims, lambda *_: (0,) * len(dims))


def tiles(width):
    return pl.BlockSpec((TILE, width), lambda i, *_: (i, 0))


def exchange(replicated):
    return lax.all_to_all(replicated, AXES, 0, 0)


def on_device(
    images, image_counts, labels, fw_picks, task_average, conv_weights, conv_momentum, conv_average,
    norm_parameter_list, norm_momentum, norm_average, head_params, head_momentum, head_average,
):
    rows, map_side, channels = images.shape[0], images.shape[1], images.shape[3]
    width = map_side * map_side * channels
    devices = lax.axis_size(AXES)
    tasks = labels.shape[1]
    fw_steps = fw_picks.shape[0]
    steps = rows // TILE
    grid = (steps,)
    stat = (devices, 8, LANES)

    def call(body, grid_, ins, outs, scratch, count=None):
        arrays = [a for a, _ in ins]
        specs = [s for _, s in ins]
        out_specs = [s for _, s in outs]
        out_shape = [a for a, _ in outs]
        spec = pltpu.PrefetchScalarGridSpec(
            num_scalar_prefetch=0 if count is None else 1, grid=grid_, in_specs=specs, out_specs=out_specs, scratch_shapes=scratch
        )
        args = arrays if count is None else [count] + arrays
        return pl.pallas_call(body, grid_spec=spec, out_shape=out_shape, compiler_params=PARAMS)(*args)

    low = conv_weights.astype(BF16)
    k1 = lax.all_gather(low[0], AXES, axis=0, tiled=True)
    k2 = lax.all_gather(low[1], AXES, axis=0, tiled=True)
    heads = lax.all_gather(head_params, "task", axis=1, tiled=True)
    heads = jnp.pad(heads, ((0, 7), (0, LANES - tasks)))
    labels = jnp.pad(labels, ((0, 0), (0, LANES - tasks)))
    flat_images = images.reshape(rows, width)
    start = jnp.pad(task_average[None, :], ((0, 7), (0, LANES - tasks)))
    basis = jnp.concatenate(
        [
            (jnp.arange(LANES, dtype=jnp.int32)[None, :] == fw_picks[:, None]).astype(F32),
            start[0:1],
            jnp.zeros((32 - fw_steps - 1, LANES), F32),
        ],
        axis=0,
    )
    norm_spec, head_spec = whole((4, channels)), whole(heads.shape)
    g1_spec, stat_spec = whole((devices, 16, LANES)), whole(stat)
    k_spec = whole((9 * channels, channels))
    acc = pltpu.VMEM((2, 8, channels), F32)

    def bind(body, *static):
        return lambda *refs: body(*static, *refs)

    first, stat1 = call(
        bind(first_kernel, steps), grid, [(flat_images, tiles(width)), (k1, k_spec)],
        [(shape((rows, width)), tiles(width)), (shape((devices, 16, LANES)), g1_spec)], [acc], image_counts,
    )
    g1 = exchange(stat1)
    hidden, second, stat2 = call(
        bind(second_kernel, steps), grid,
        [(first, tiles(width)), (g1, g1_spec), (norm_parameter_list, norm_spec), (k2, k_spec)],
        [(shape((rows, width), BF16), tiles(width)), (shape((rows, width)), tiles(width)), (shape(stat), stat_spec)], [acc], image_counts,
    )
    g2 = exchange(stat2)
    block_flat, slope, slope_sum, slope_xhat, pooled, resid, gram = call(
        bind(head_kernel, steps, tasks), grid,
        [(second, tiles(width)), (g2, stat_spec), (g1, g1_spec), (norm_parameter_list, norm_spec), (flat_images, tiles(width)),
         (labels, tiles(LANES)), (heads, head_spec), (basis, whole(basis.shape))],
        [(shape((rows, width), BF16), tiles(width)), (shape((rows, width)), tiles(width)), (shape((rows, channels)), tiles(channels)),
         (shape((rows, channels)), tiles(channels)), (shape((rows, channels + LANES)), tiles(channels + LANES)),
         (shape((rows, LANES)), tiles(LANES)), (shape(stat), stat_spec)],
        [pltpu.VMEM((LANES, LANES), F32)], image_counts,
    )
    g3 = exchange(gram)
    dout, stat4, head_partial, mix = call(
        bind(mix_kernel, steps, fw_steps), grid,
        [(g3, stat_spec), (basis, whole(basis.shape)), (start, whole(start.shape)), (resid, tiles(LANES)),
         (pooled, tiles(channels + LANES)), (heads, head_spec), (slope_sum, tiles(channels)), (slope_xhat, tiles(channels))],
        [(shape((rows, channels)), tiles(channels)), (shape(stat), stat_spec),
         (shape((LANES, channels + LANES)), whole((LANES, channels + LANES))), (shape((8, LANES)), whole((8, LANES)))],
        [acc],
    )
    g4 = exchange(stat4)
    dsecond, dnormed, stat5 = call(
        bind(back_second_kernel, steps), grid,
        [(slope, tiles(width)), (dout, tiles(channels)), (second, tiles(width)), (first, tiles(width)), (g1, g1_spec),
         (g2, stat_spec), (g4, stat_spec), (norm_parameter_list, norm_spec), (k2, k_spec)],
        [(shape((rows, width), BF16), tiles(width)), (shape((rows, width)), tiles(width)), (shape(stat), stat_spec)], [acc], image_counts,
    )
    g5 = exchange(stat5)
    halves = 2
    part = channels // halves

    def weight_grad(x, d):
        return call(
            weight_grad_kernel, (halves,),
            [(x, whole((rows, width)))] + [(d, pl.BlockSpec((rows, part), lambda i, p=p: (0, p * halves + i))) for p in range(4)],
            [(shape((9 * channels, channels)), pl.BlockSpec((9 * channels, part), lambda i: (0, i)))], [],
        )[0]

    grad_two = lax.psum_scatter(weight_grad(hidden, dsecond), AXES, scatter_dimension=0, tiled=True)
    (dfirst,) = call(
        dfirst_kernel, grid,
        [(dnormed, tiles(width)), (first, tiles(width)), (g1, g1_spec), (g5, stat_spec), (norm_parameter_list, norm_spec)],
        [(shape((rows, width), BF16), tiles(width))], [], image_counts,
    )
    grad_one = lax.psum_scatter(weight_grad(flat_images, dfirst), AXES, scatter_dimension=0, tiled=True)
    (image_flat,) = call(
        image_grad_kernel, grid,
        [(dfirst, tiles(width)), (k1, k_spec), (slope, tiles(width)), (dout, tiles(channels))],
        [(shape((rows, width)), tiles(width))], [],
    )
    task_cols = head_params.shape[1]
    ways = tasks // task_cols
    send = head_partial[:tasks].reshape(1, ways, task_cols, -1)
    send = jnp.broadcast_to(send, (devices // ways,) + send.shape[1:]).reshape(devices, task_cols, -1)
    head_grads = jnp.sum(exchange(send), 0)[:, : channels + 1].T
    task_average_new = AVERAGE_DECAY * task_average + (1.0 - AVERAGE_DECAY) * mix[0, :tasks]
    sums4 = jnp.sum(g4, 0).reshape(2, channels)
    sums5 = jnp.sum(g5, 0).reshape(2, channels)
    norm_grads = jnp.concatenate([sums5, sums4], axis=0)
    conv_grads = jnp.stack([grad_one, grad_two])
    conv_momentum_new, conv_weights_new, conv_average_new = nesterov(conv_weights, conv_momentum, conv_grads, CONV_RATE, conv_average)
    norm_momentum_new, norm_params_new, norm_average_new = nesterov(
        norm_parameter_list, norm_momentum, norm_grads, NORM_RATE, norm_average
    )
    head_momentum_new, head_params_new, head_average_new = nesterov(head_params, head_momentum, head_grads, HEAD_RATE, head_average)
    return (
        block_flat.reshape(images.shape),
        image_flat.reshape(images.shape),
        conv_grads,
        conv_momentum_new,
        conv_weights_new,
        conv_average_new,
        conv_weights_new.astype(BF16),
        norm_grads,
        norm_momentum_new,
        norm_params_new,
        norm_average_new,
        head_grads,
        head_momentum_new,
        head_params_new,
        head_average_new,
        task_average_new,
    )


def solution(mesh):
    both = P(AXES)
    rowwise = P(None, AXES, None)
    head = P(None, "task")
    return jax.shard_map(
        on_device,
        mesh=mesh,
        in_specs=(both, both, both, P(), P(), rowwise, rowwise, rowwise, P(), P(), P(), head, head, head),
        out_specs=(both, both, rowwise, rowwise, rowwise, rowwise, rowwise, P(), P(), P(), P(), head, head, head, head, P()),
        check_vma=False,
    )
```

time: 1080 us -> 569 us (0.53)
  blocking collectives: 207 us -> 28 us
  matrix products: 170 us -> 0 us
  other arithmetic: 176 us -> 7.87 us
  Pallas kernels: 0 us -> 132 us
  local copies, waits for them, and re-layouts: 120 us -> 35.8 us
  loops' own time: 65.9 us -> 0 us
  waiting for transfers between devices: 317 us -> 335 us
  starting transfers between devices: 0.08 us -> 15.1 us
    psum x1 -> x0, waiting for transfers between devices: 258 us -> none  [on_device(): summed = lax.psum(local_grads, ('dp', 'task'))]
    psum x5 -> x0, blocking collectives: 200 us -> none  [the longest x1 40.4 us: on_device(): lax.psum((second_norm_shift, second_norm_gain, head_partial), ('dp', 'tas...]
    reduce_scatter x0 -> x2, waiting for transfers between devices: none -> 199 us  [the longest x1 141 us: on_device(): lax.psum_scatter(weight_grad(flat_images, dfirst), AXES, scatter_dimensio...]
    dot_general x51 -> x0, matrix products: 170 us -> none  [the longest x20 28 us: frank_step(): gram_mix = jnp.dot(gram_matrix, task_mix, precision=PRECISE)]
    pallas_call x0 -> x9, Pallas kernels: none -> 132 us  [call(): pl.pallas_call(body, grid_spec=spec, out_shape=out_shape, compiler_params...]
    concatenate x3 -> x1, other arithmetic: 86.2 us -> 0.68 us  [on_device(): jnp.concatenate([(jnp.arange(LANES, dtype=jnp.int32)[None, :] == fw_picks...]
    another operation x1 -> x0, loops' own time: 65.9 us -> none  [frank_wolfe(): final_mix, unused = lax.scan(frank_step, start_mix, vertex_ids)]
    all_gather x1 -> x2, waiting for transfers between devices: 59.5 us -> 110 us  [the longest x1 59.6 us: on_device(): k1 = lax.all_gather(low[0], AXES, axis=0, tiled=True)]
  transfers between devices with their start and end apart: 2 -> 8, of which waited for: 2 -> 6; matrix products, arithmetic and copies ran while one was open for 7% -> 6% of each run, Pallas kernels for 0% -> 10%
where the time goes in v1:
time: 569 us; the launch traced here: 568 us
  waiting for transfers between devices  335 us (59%)
  Pallas kernels  132 us (23%)
  local copies, waits for them, and re-layouts  35.8 us (6%)
  blocking collectives  28 us (5%)
  starting transfers between devices  15.1 us (3%)
  between operations  14.6 us (3%)
  other arithmetic  7.87 us (1%)
    reduce_scatter x1, waiting for transfers between devices, on_device(): lax.psum_scatter(weight_grad(flat_images, dfirst), AXES, scatter_dimensio...  141 us
    pallas_call x9, Pallas kernels, call(): pl.pallas_call(body, grid_spec=spec, out_shape=out_shape, compiler_params...  132 us
    all_gather x1, waiting for transfers between devices, on_device(): k1 = lax.all_gather(low[0], AXES, axis=0, tiled=True)  59.6 us
    reduce_scatter x1, waiting for transfers between devices, on_device(): lax.psum_scatter(weight_grad(hidden, dsecond), AXES, scatter_dimension=0,...  57.5 us
    all_gather x1, waiting for transfers between devices, on_device(): k2 = lax.all_gather(low[1], AXES, axis=0, tiled=True)  49.9 us
    all_to_all x4, waiting for transfers between devices, exchange(): return lax.all_to_all(replicated, AXES, 0, 0)  25.7 us
    all_to_all x2, blocking collectives, exchange(): return lax.all_to_all(replicated, AXES, 0, 0)  22.1 us
    all_to_all x4, starting transfers between devices, exchange(): return lax.all_to_all(replicated, AXES, 0, 0)  14.9 us
  transfers between devices with their start and end apart: 8, of which 6 were waited for; matrix products, arithmetic and copies ran while one was open for 6% of the time, Pallas kernels for 10%

profile of v1, /device:TPU:0, one launch (start us, length us, event | category | flops | bytes accessed | tf_op | source)
XLA Modules:
  0.0 568.1 jit_solution(10500443030363139122)
XLA Ops:
  7.2 1.1 convert_element_type.13
  10.5 7.8 %reshape.53.refs_1_.refs_5_.x_ref = bf16[1024,2048]{1,0:T(8,128)(2,1)} reshape(bf16[1024,2,2,512]{3,2,1,0:T(2,128)(2,1)} %param.14) | data formatting | bytes 8388608 | tf_op jit(solution)/shard_map/reshape | solution.py:390
  18.3 59.6 %all-gather.6.cloned.1.call-done = bf16[1,4608,512]{2,1,0:T(8,128)(2,1)} async-done(((bf16[1,144,512]{2,1,0:T(8,128)(2,1)}), bf16[1,4608,512]{2,1,0:T(8,128)(2,1)}) %all-gather.6.cloned.1.call-update) | async-done | bytes 4718608 | tf_op jit(solution)/shard_map/all_gather | solution.py:385
  77.9 13.7 %shard_map.261 = (f32[1024,2048]{1,0:T(8,128)}, f32[32,16,128]{2,1,0:T(8,128)}) custom-call(s32[1]{0:T(128)S(6)} %copy.44.refs_0_.count_ref, bf16[1024,2048]{1,0:T(8,128)(2,1)} %reshape.53.refs_1_.refs_5_.x_ref, bf16[4608,512]{1,0:T(8,128)(2,1)} %bitcast.19), custom_call_target="tpu_custom_call" | custom-call | tf_op jit(solution)/shard_map/pallas_call | solution.py:382
  91.6 3.4 all-to-all-start
  95.1 49.9 %all-gather.8.cloned.1.call-done = bf16[1,4608,512]{2,1,0:T(8,128)(2,1)} async-done(((bf16[1,144,512]{2,1,0:T(8,128)(2,1)}), bf16[1,4608,512]{2,1,0:T(8,128)(2,1)}) %all-gather.8.cloned.1.call-update) | async-done | bytes 4718608 | tf_op jit(solution)/shard_map/all_gather | solution.py:386
  145.7 15.8 %shard_map.262 = (bf16[1024,2048]{1,0:T(8,128)(2,1)}, f32[1024,2048]{1,0:T(8,128)}, f32[32,8,128]{2,1,0:T(8,128)}) custom-call(s32[1]{0:T(128)S(6)} %copy.44.refs_0_.count_ref, f32[1024,2048]{1,0:T(8,128)} %get-tuple-element.35.refs_1_.refs_4_.first_ref, f32[32,16,128]{2,1,0:T(8,128)} %copy-done, f32[4,512]{1,0:T(4,128)} %norm_ref.1, bf16[4608,512]{1,0:T(8,128)(2,1)} %bitcast.17), custom_call_target="tpu_custom_call" | custom-call | tf_op jit(solution)/shard_map/pallas_call | solution.py:382
  161.5 3.4 all-to-all-start.1
  164.9 5.9 %all-gather.2 = f32[4,10,513]{2,1,0:T(8,128)S(1)} all-gather(f32[1,10,513]{2,1,0:T(8,128)S(1)} %bitcast.24), channel_id=1, replica_groups=mesh['dp'=8,'task'=4] {'task'}, dimensions={0}, use_global_device_ids=true | all-gather | bytes 102600 | tf_op jit(solution)/shard_map/all_gather | solution.py:387
  172.0 0.8 pad.12.refs_6_
  174.2 18.8 %shard_map.263 = (bf16[1024,2048]{1,0:T(8,128)(2,1)}, f32[1024,2048]{1,0:T(8,128)}, f32[1024,512]{1,0:T(8,128)}, f32[1024,512]{1,0:T(8,128)}, f32[1024,640]{1,0:...) custom-call(s32[1]{0:T(128)S(6)} %copy.44.refs_0_.count_ref, f32[1024,2048]{1,0:T(8,128)} %get-tuple-element.37.refs_1_.refs_3_, ...), custom_call_target="tpu_custom_call" | custom-call | tf_op jit(solution)/shard_map/pallas_call | solution.py:382
  193.0 5.4 all-to-all-start.2
  199.1 7.6 %all-to-all-done.2.refs_0_ = f32[32,8,128]{2,1,0:T(8,128)S(1)} async-done(((f32[32,8,128]{2,1,0:T(8,128)}), f32[32,8,128]{2,1,0:T(8,128)S(1)}, u32[]{:S(2)}, u32[]{:S(2)}) %all-to-all-start.2) | async-done | bytes 131104 | tf_op jit(solution)/shard_map/all_to_all | solution.py:357
  207.3 8.3 %shard_map.264 = (f32[1024,512]{1,0:T(8,128)}, f32[32,8,128]{2,1,0:T(8,128)}, f32[128,640]{1,0:T(8,128)}, f32[8,128]{1,0:T(8,128)}) custom-call(f32[32,8,128]{2,1,0:T(8,128)} %copy-done.8, f32[32,128]{1,0:T(8,128)} %maximum_maximum_fusion.refs_8_.refs_1_, f32[8,128]{1,0:T(8,128)} %pad.14.refs_2_, f32[1024,128]{1,0:T(8,128)} %get-tuple-element.42.refs_3_, ...), custom_call_target="tpu_custom_call" | custom-call | tf_op jit(solution)/shard_map/pallas_call | solution.py:382
  215.6 11.5 %all_to_all.30.refs_7_ = f32[32,8,128]{2,1,0:T(8,128)} all-to-all(f32[32,8,128]{2,1,0:T(8,128)} %get-tuple-element.47), channel_id=1, replica_groups=mesh['dp'=8,'task'=4] {'dp','task'}, dimensions={0} | all-to-all | bytes 262144 | tf_op jit(solution)/shard_map/all_to_all | solution.py:357
  227.1 20.1 %shard_map.265 = (bf16[1024,2048]{1,0:T(8,128)(2,1)}, f32[1024,2048]{1,0:T(8,128)}, f32[32,8,128]{2,1,0:T(8,128)}) custom-call(s32[1]{0:T(128)S(6)} %copy.44.refs_0_.count_ref, f32[1024,2048]{1,0:T(8,128)} %get-tuple-element.40.refs_1_.slope_ref, f32[1024,512]{1,0:T(8,128)} %get-tuple-element.46.refs_2_.dout_ref, ...), custom_call_target="tpu_custom_call" | custom-call | tf_op jit(solution)/shard_map/pallas_call | solution.py:382
  247.2 14.7 %shard_map.269 = f32[4608,512]{1,0:T(8,128)} custom-call(bf16[1024,2048]{1,0:T(8,128)(2,1)} %get-tuple-element.50.x_ref, bf16[1024,2048]{1,0:T(8,128)(2,1)} %get-tuple-element.51.d0_ref.d1_ref.d2_ref.d3_ref, bf16[1024,2048]{1,0:T(8,128)(2,1)} %get-tuple-element.51.d0_ref.d1_ref.d2_ref.d3_ref, ...), custom_call_target="tpu_custom_call" | custom-call | tf_op jit(solution)/shard_map/pallas_call | solution.py:382
  262.9 10.6 %all_to_all.31.g5_ref = f32[32,8,128]{2,1,0:T(8,128)} all-to-all(f32[32,8,128]{2,1,0:T(8,128)S(1)} %copy-done.12), channel_id=1, replica_groups=mesh['dp'=8,'task'=4] {'dp','task'}, dimensions={0} | all-to-all | bytes 262144 | tf_op jit(solution)/shard_map/all_to_all | solution.py:357
  273.5 10.0 %shard_map.266.dfirst_ref.d0_ref.d1_ref.d2_ref.d3_ref = bf16[1024,2048]{1,0:T(8,128)(2,1)} custom-call(s32[1]{0:T(128)S(6)} %copy.44.refs_0_.count_ref, f32[1024,2048]{1,0:T(8,128)} %get-tuple-element.48.dnormed_ref, f32[1024,2048]{1,0:T(8,128)} %get-tuple-element.35.refs_1_.refs_4_.first_ref, f32[32,16,128]{2,1,0:T(8,128)} %copy-done, ...), custom_call_target="tpu_custom_call" | custom-call | tf_op jit(solution)/shard_map/pallas_call | solution.py:382
  283.5 15.0 %shard_map.268 = f32[4608,512]{1,0:T(8,128)} custom-call(bf16[1024,2048]{1,0:T(8,128)(2,1)} %reshape.53.refs_1_.refs_5_.x_ref, bf16[1024,2048]{1,0:T(8,128)(2,1)} %shard_map.266.dfirst_ref.d0_ref.d1_ref.d2_ref.d3_ref, bf16[1024,2048]{1,0:T(8,128)(2,1)} %shard_map.266.dfirst_ref.d0_ref.d1_ref.d2_ref.d3_ref, ...), custom_call_target="tpu_custom_call" | custom-call | tf_op jit(solution)/shard_map/pallas_call | solution.py:382
  298.5 0.9 slice.21
  299.4 1.2 broadcast_in_dim.18
  300.6 2.7 all-to-all-start.5
  303.3 7.8 %reshape.54 = bf16[1024,2,2,512]{3,2,1,0:T(2,128)(2,1)} reshape(bf16[1024,2048]{1,0:T(8,128)(2,1)} %get-tuple-element.39) | data formatting | bytes 8388608 | tf_op jit(solution)/shard_map/reshape | solution.py:483
  311.1 1.2 fusion.1
  312.4 15.4 %shard_map.267 = f32[1024,2048]{1,0:T(8,128)} custom-call(bf16[1024,2048]{1,0:T(8,128)(2,1)} %shard_map.266.dfirst_ref.d0_ref.d1_ref.d2_ref.d3_ref, bf16[4608,512]{1,0:T(8,128)(2,1)} %bitcast.20, f32[1024,2048]{1,0:T(8,128)} %get-tuple-element.40.refs_1_.slope_ref, f32[1024,512]{1,0:T(8,128)} %get-tuple-element.46.refs_2_.dout_ref), custom_call_target="tpu_custom_call" | custom-call | tf_op jit(solution)/shard_map/pallas_call | solution.py:382
  327.9 11.8 %reshape.55 = f32[1024,2,2,512]{3,2,1,0:T(2,128)} reshape(f32[1024,2048]{1,0:T(8,128)} %shard_map.267) | data formatting | bytes 16777216 | tf_op jit(solution)/shard_map/reshape | solution.py:484
  340.4 18.2 %all-to-all-done.5 = f32[32,10,640]{2,1,0:T(8,128)S(1)} async-done(((f32[32,10,640]{2,1,0:T(8,128)}), f32[32,10,640]{2,1,0:T(8,128)S(1)}, u32[]{:S(2)}, u32[]{:S(2)}) %all-to-all-start.5) | async-done | bytes 819232 | tf_op jit(solution)/shard_map/all_to_all | solution.py:357
  359.3 57.5 %reduce-scatter.5.cloned.1.call-done = f32[144,512]{1,0:T(8,128)} async-done(((f32[4608,512]{1,0:T(8,128)}), f32[144,512]{1,0:T(8,128)}) %reduce-scatter.5.cloned.1.call-update) | async-done | bytes 294928 | tf_op jit(solution)/shard_map/reduce_scatter | solution.py:455
  416.8 141.4 %reduce-scatter.3.cloned.1.call-done = f32[144,512]{1,0:T(8,128)} async-done(((f32[4608,512]{1,0:T(8,128)}), f32[144,512]{1,0:T(8,128)}) %reduce-scatter.3.cloned.1.call-update) | async-done | bytes 294928 | tf_op jit(solution)/shard_map/reduce_scatter | solution.py:461
  558.2 2.4 fusion.2
  560.6 1.0 add_multiply_fusion
  (67 shorter events, 8.5 us)
Async XLA Ops:
  7.2 70.7 %all-gather.6.cloned.1.call-start = ((), (), s32[]{:S(2)}) async-start(), calls=%async_computation.10 | async-start | bytes 4866048 | tf_op jit(solution)/shard_map/all_gather | solution.py:385
  9.1 135.9 %all-gather.8.cloned.1.call-start = ((), (), s32[]{:S(2)}) async-start(), calls=%async_computation.11 | async-start | bytes 4866048 | tf_op jit(solution)/shard_map/all_gather | solution.py:386
  77.9 17.1 %copy-start.18 = (f32[40]{0:T(128)S(1)}, f32[40]{0:T(128)}, u32[]{:S(2)}) copy-start(f32[40]{0:T(128)} %param.18) | copy-start | bytes 484
  77.9 17.1 %copy-start.17 = (s32[20]{0:T(128)S(1)}, s32[20]{0:T(128)}, u32[]{:S(2)}) copy-start(s32[20]{0:T(128)} %param.17) | copy-start | bytes 244
  91.6 53.4 %all-to-all-start = ((f32[32,16,128]{2,1,0:T(8,128)}), f32[32,16,128]{2,1,0:T(8,128)S(1)}, u32[]{:S(2)}, u32[]{:S(2)}) async-start(f32[32,16,128]{2,1,0:T(8,128)} %get-tuple-element.36), calls=%async_computation | async-start | bytes 524288 | tf_op jit(solution)/shard_map/all_to_all | solution.py:357
  145.0 0.7 copy-start
  145.7 19.2 %copy-start.10 = (f32[513,10]{0,1:T(8,128)S(1)}, f32[513,10]{0,1:T(8,128)}, u32[]{:S(2)}) copy-start(f32[513,10]{0,1:T(8,128)} %param.25) | copy-start | bytes 61564
  145.7 25.3 %copy-start.11 = (s32[1024,40]{0,1:T(8,128)S(1)}, s32[1024,40]{0,1:T(8,128)}, u32[]{:S(2)}) copy-start(s32[1024,40]{0,1:T(8,128)} %param.16) | copy-start | bytes 491524
  161.5 12.0 %all-to-all-start.1 = ((f32[32,8,128]{2,1,0:T(8,128)}), f32[32,8,128]{2,1,0:T(8,128)S(1)}, u32[]{:S(2)}, u32[]{:S(2)}) async-start(f32[32,8,128]{2,1,0:T(8,128)} %get-tuple-element.38), calls=%async_computation.1 | async-start | bytes 262144 | tf_op jit(solution)/shard_map/all_to_all | solution.py:357
  173.5 0.7 copy-start.3
  193.0 13.7 %all-to-all-start.2 = ((f32[32,8,128]{2,1,0:T(8,128)}), f32[32,8,128]{2,1,0:T(8,128)S(1)}, u32[]{:S(2)}, u32[]{:S(2)}) async-start(f32[32,8,128]{2,1,0:T(8,128)} %get-tuple-element.41), calls=%async_computation.2 | async-start | bytes 262144 | tf_op jit(solution)/shard_map/all_to_all | solution.py:357
  198.5 218.4 %reduce-scatter.5.cloned.1.call-start = ((), (), s32[]{:S(2)}) async-start(), calls=%async_computation.9 | async-start | bytes 9732096 | tf_op jit(solution)/shard_map/reduce_scatter | solution.py:455
  206.7 0.6 copy-start.8
  262.0 0.9 copy-start.12
  262.0 296.2 %reduce-scatter.3.cloned.1.call-start = ((), (), s32[]{:S(2)}) async-start(), calls=%async_computation.8 | async-start | bytes 9732096 | tf_op jit(solution)/shard_map/reduce_scatter | solution.py:461
  300.6 57.9 %all-to-all-start.5 = ((f32[32,10,640]{2,1,0:T(8,128)}), f32[32,10,640]{2,1,0:T(8,128)S(1)}, u32[]{:S(2)}, u32[]{:S(2)}) async-start(f32[32,10,640]{2,1,0:T(8,128)} %bitcast.8), calls=%async_computation.7 | async-start | bytes 2621440 | tf_op jit(solution)/shard_map/all_to_all | solution.py:357
  303.3 9.1 %copy-start.4 = (f32[32,8,128]{2,1,0:T(8,128)S(1)}, f32[32,8,128]{2,1,0:T(8,128)}, u32[]{:S(2)}) copy-start(f32[32,8,128]{2,1,0:T(8,128)} %all_to_all.30.refs_7_) | copy-start | bytes 393220
  312.4 15.4 %copy-start.5 = (f32[32,8,128]{2,1,0:T(8,128)S(1)}, f32[32,8,128]{2,1,0:T(8,128)}, u32[]{:S(2)}) copy-start(f32[32,8,128]{2,1,0:T(8,128)} %all_to_all.31.g5_ref) | copy-start | bytes 393220
  327.8 11.9 %copy-start.9 = (f32[4,512]{1,0:T(4,128)S(1)}, f32[4,512]{1,0:T(4,128)}, u32[]{:S(2)}) copy-start(f32[4,512]{1,0:T(4,128)} %norm_ref.1) | copy-start | bytes 24580
  327.8 11.9 %copy-start.15 = (f32[4,512]{1,0:T(4,128)S(1)}, f32[4,512]{1,0:T(4,128)}, u32[]{:S(2)}) copy-start(f32[4,512]{1,0:T(4,128)} %param.24) | copy-start | bytes 24580
  327.8 11.9 %copy-start.16 = (f32[4,512]{1,0:T(4,128)S(1)}, f32[4,512]{1,0:T(4,128)}, u32[]{:S(2)}) copy-start(f32[4,512]{1,0:T(4,128)} %param.23) | copy-start | bytes 24580
  327.8 30.8 %copy-start.13 = (f32[513,10]{0,1:T(8,128)S(1)}, f32[513,10]{0,1:T(8,128)}, u32[]{:S(2)}) copy-start(f32[513,10]{0,1:T(8,128)} %param.27) | copy-start | bytes 61564
  327.8 30.8 %copy-start.14 = (f32[513,10]{0,1:T(8,128)S(1)}, f32[513,10]{0,1:T(8,128)}, u32[]{:S(2)}) copy-start(f32[513,10]{0,1:T(8,128)} %param.26) | copy-start | bytes 61564
  327.9 230.4 %copy-start.2 = (f32[2,144,512]{2,1,0:T(8,128)S(1)}, f32[2,144,512]{2,1,0:T(8,128)}, u32[]{:S(2)}) copy-start(f32[2,144,512]{2,1,0:T(8,128)} %param.19) | copy-start | bytes 1769476
  327.9 230.4 %copy-start.7 = (f32[2,144,512]{2,1,0:T(8,128)S(1)}, f32[2,144,512]{2,1,0:T(8,128)}, u32[]{:S(2)}) copy-start(f32[2,144,512]{2,1,0:T(8,128)} %param.20) | copy-start | bytes 1769476
  339.7 220.9 %copy-start.6 = (f32[2,144,512]{2,1,0:T(8,128)S(1)}, f32[2,144,512]{2,1,0:T(8,128)}, u32[]{:S(2)}) copy-start(f32[2,144,512]{2,1,0:T(8,128)} %param.21) | copy-start | bytes 1769476
  560.6 1.0 copy-start.1
Sparse Core Ops, SparseCore 0:
  11.5 66.3 all-gather.5
  81.3 63.6 all-gather.7
  262.1 154.6 reduce-scatter.4
  423.6 134.5 reduce-scatter.2
